TPU v7x, 32 devices: a whole 2x2x4 slice. The times are simulated.
32 devices in a mesh: groups: 2 (over x), row: 4 (over z), col: 4 (over y, core).
Axes of the slice: x: 2, y: 2, z: 4, core: 2. Of those that a mesh axis runs over, the one named last changes fastest.
Arguments:
- probes: bfloat16 [1024, 2048], P('groups', ('row', 'col')), parts along dimension 0, may hold values from -6 to 6
- ham_blocks: bfloat16 [32, 4, 2, 128, 128], P(('groups', 'row', 'col')), parts along dimension 0, as said below
- strain_blocks: bfloat16 [32, 4, 2, 6, 128, 128], P(('groups', 'row', 'col')), parts along dimension 0, as said below
- block_cols: int32 [32, 4, 2], P(('groups', 'row', 'col')), parts along dimension 0, may hold values from -1 to 15, as said below
- odd_coeffs: float32 [2], replicated, may hold values from 0.5 to 1.5
Outputs:
- density: bfloat16 [1024, 2048], P('groups', ('col', 'row')), parts along dimension 0
- stress: float32 [12, 16], P('groups', 'row'), parts along dimension 0
There are 2 independent parts, one for each index of `groups`. A program takes and returns all parts, laid end to end along the dimension named above; an argument that names none is the same for every part. Nothing has to cross between parts.
Inputs may be any that keep to these rules, and one draw needn't show every extreme that they name: block_cols[i,g,s] is -1 or a block column of group g (from g * 4 to g * 4 + 3); the filled slots of a group come first and name distinct columns; every block row has exactly 2 filled slots in its own group (the one holding column i); the pattern is symmetric: column j is named in row i exactly when column i is named in row j. `ham_blocks`: the slot of an empty block_cols entry holds zeros; block (j, i) is the transpose of block (i, j), so H is symmetric. `strain_blocks`: the slot of an empty block_cols entry holds zeros; block (j, i) is the transpose of block (i, j) in every component.
All inputs are finite; a program needn't handle non-finite values.
Results may differ from a plain program's by a relative error of at most 0.023.
Values may be sent and summed in bfloat16 or wider, within the bound.
A program may use at most 128 MiB of HBM per device.

v0:
```python
import jax
import jax.numpy as jnp
from jax import lax
from jax.sharding import PartitionSpec as P


def along_row(panel):
    return lax.all_gather(panel, "col", axis=1, tiled=True)


def along_col(panel):
    return lax.all_gather(panel, "row", axis=1, tiled=True)


def down_sum(partial_value):
    return lax.psum_scatter(
        partial_value.astype(jnp.bfloat16), "row", scatter_dimension=1, tiled=True
    ).astype(jnp.float32)


def local(probes, ham_blocks, strain_blocks, block_cols, odd_coeffs):
    probe_count = probes.shape[0]
    block_size = ham_blocks.shape[-1]
    own_rows = probes.shape[1] // block_size
    components = strain_blocks.shape[3]
    ham_local, strain_local, cols_local = (
        lax.all_to_all(ham_blocks, "col", split_axis=1, concat_axis=0, tiled=True),
        lax.all_to_all(strain_blocks, "col", split_axis=1, concat_axis=0, tiled=True),
        lax.all_to_all(block_cols, "col", split_axis=1, concat_axis=0, tiled=True),
    )
    grid_rows = ham_local.shape[0]
    slot_cap = ham_local.shape[2]
    slot_count = grid_rows * slot_cap
    ham_slots = ham_local.reshape(slot_count, block_size, block_size)
    col_slots = cols_local.reshape(slot_count)
    group_width = lax.axis_size("row") * own_rows
    local_cols = col_slots - lax.axis_index("col") * group_width
    filled = col_slots >= 0
    safe_cols = jnp.clip(local_cols, 0, group_width - 1).astype(jnp.int32)
    placement = (
        (safe_cols[:, None] == jnp.arange(group_width, dtype=jnp.int32)[None, :]) & filled[:, None]
    ).astype(jnp.float32)

    def backward(gathered):
        spread = jnp.repeat(gathered.reshape(probe_count, grid_rows, block_size), slot_cap, axis=1)
        contrib = jnp.einsum("psa,sab->psb", spread, ham_slots, preferred_element_type=jnp.float32)
        placed = jnp.einsum("psb,sj->pjb", contrib, placement, precision=lax.Precision.HIGHEST)
        return placed.reshape(probe_count, group_width * block_size)

    probes_row = along_row(probes)
    first_term = down_sum(backward(probes_row)).astype(jnp.bfloat16)
    first_col = along_col(first_term)
    picked = jnp.take(first_col.reshape(probe_count, group_width, block_size), safe_cols, axis=1)
    contrib = jnp.einsum("psb,sab->psa", picked, ham_slots, preferred_element_type=jnp.float32)
    summed = contrib.reshape(probe_count, grid_rows, slot_cap, block_size).sum(axis=2)
    partial_two = summed.reshape(probe_count, grid_rows * block_size)
    row_piece = lax.psum_scatter(
        partial_two.astype(jnp.bfloat16), "col", scatter_dimension=1, tiled=True
    ).astype(jnp.float32)
    second_term = (2.0 * row_piece - probes.astype(jnp.float32)).astype(jnp.bfloat16)
    second_row = along_row(second_term)
    third_term = 2.0 * down_sum(backward(second_row)) - first_term.astype(jnp.float32)
    density = (odd_coeffs[0] * first_term.astype(jnp.float32) + odd_coeffs[1] * third_term).astype(
        jnp.bfloat16
    )
    density_col = along_col(density)
    own_probes = jnp.repeat(
        probes_row.reshape(probe_count, grid_rows, block_size), slot_cap, axis=1
    )
    others = jnp.take(density_col.reshape(probe_count, group_width, block_size), safe_cols, axis=1)
    pair_tiles = jnp.einsum(
        "psa,psb->sab", own_probes, others, preferred_element_type=jnp.float32
    ).astype(jnp.bfloat16)
    strain_slots = strain_local.reshape(slot_count, components, block_size, block_size)
    slot_terms = jnp.einsum(
        "skab,sab->ks", strain_slots, pair_tiles, preferred_element_type=jnp.float32
    )
    row_terms = slot_terms.reshape(components, grid_rows, slot_cap).sum(axis=2) / probe_count
    stress = lax.psum(row_terms, "col")
    return (density, stress)


def solution(mesh):
    placed = (
        P("groups", ("row", "col")),
        P(("groups", "row", "col"), None, None, None, None),
        P(("groups", "row", "col"), None, None, None, None, None),
        P(("groups", "row", "col"), None, None),
        P(),
    )
    return jax.shard_map(
        local,
        mesh=mesh,
        in_specs=placed,
        out_specs=(P("groups", ("col", "row")), P("groups", "row")),
        check_vma=False,
    )
```

profile of v0, /device:TPU:0, one launch (start us, length us, event | category | flops | bytes accessed | tf_op | source)
XLA Modules:
  0.0 170.8 jit_solution(3243459258350022473)
XLA Ops:
  7.2 1.3 copy.44
  8.5 4.2 %all-to-all-start = ((s32[1,4,2]{2,0,1:T(1,128)}), s32[1,4,2]{2,0,1:T(1,128)S(1)}, u32[]{:S(2)}, u32[]{:S(2)}) async-start(s32[1,4,2]{2,0,1:T(1,128)} %copy.44), calls=%async_computation | async-start | bytes 4096 | tf_op jit(solution)/shard_map/all_to_all | solution.py:29
  12.7 7.9 %all_gather.12 = bf16[512,512]{1,0:T(8,128)(2,1)S(1)} all-gather(bf16[512,128]{1,0:T(8,128)(2,1)} %param.7), channel_id=1, replica_groups=mesh['groups'=2,'row'=4,'col'=4] {'col'}, dimensions={1}, use_global_device_ids=true | all-gather | bytes 655360 | tf_op jit(solution)/shard_map/all_gather | solution.py:8
  20.6 0.1 copy_bitcast_fusion
  20.7 0.0 all-to-all-done
  20.7 3.4 %all-to-all-start.1 = ((bf16[1,4,2,128,128]{4,3,2,0,1:T(8,128)(2,1)}), bf16[1,4,2,128,128]{4,3,2,0,1:T(8,128)(2,1)S(1)}, u32[]{:S(2)}, u32[]{:S(2)}) async-start(bf16[1,4,2,128,128]{4,3,2,0,1:T(8,128)(2,1)} %bitcast.77), calls=%async_computation.1 | async-start | bytes 524288 | tf_op jit(solution)/shard_map/all_to_all | solution.py:27
  24.2 0.0 reduce-scatter.4.cloned.1.call-start
  24.2 0.1 min.12
  24.4 0.1 ge.15
  24.4 5.7 %all-to-all-done.1 = bf16[1,4,2,128,128]{4,3,2,0,1:T(8,128)(2,1)S(1)} async-done(((bf16[1,4,2,128,128]{4,3,2,0,1:T(8,128)(2,1)}), bf16[1,4,2,128,128]{4,3,2,0,1:T(8,128)(2,1)S(1)}, u32[]{:S(2)}, u32[]{:S(2)}) %all-to-all-start.1) | async-done | bytes 262176 | tf_op jit(solution)/shard_map/all_to_all | solution.py:27
  30.2 0.1 broadcast_in_dim.19
  30.3 1.8 %convolution_bitcast_fusion.1 = f32[512,8,128]{0,2,1:T(8,128)} fusion(bf16[8,128,128]{2,1,0:T(8,128)(2,1)S(1)} %bitcast.68, bf16[512,8,128]{2,0,1:T(8,128)(2,1)S(1)} %bitcast.65), kind=kOutput, calls=%fused_computation.8 | convolution fusion | flops 134217728 | bytes 3407872 | tf_op jit(solution)/shard_map/psa,sab->psb/dot_general | solution.py:46
  32.2 2.1 %copy.48 = f32[512,8,128]{2,1,0:T(8,128)S(1)} copy(f32[512,8,128]{0,2,1:T(8,128)} %convolution_bitcast_fusion.1) | data formatting | bytes 4194304 | tf_op jit(solution)/shard_map/psa,sab->psb/transpose | solution.py:46
  34.3 1.9 %fusion.7 = bf16[512,4,128]{2,1,0:T(4,128)(2,1)} fusion(f32[512,8,128]{2,1,0:T(8,128)S(1)} %copy.48, s32[8]{0:T(128)S(1)} %min.12, pred[8]{0:T(512)(128)(4,1)S(1)} %ge.15), kind=kOutput, calls=%fused_computation.11 | convolution fusion | flops 25428032 | bytes 2621480 | tf_op jit(solution)/shard_map/psb,sj->pjb/dot_general | solution.py:47
  36.2 2.1 %copy.68 = bf16[512,4,128]{0,2,1:T(8,128)(2,1)} copy(bf16[512,4,128]{2,1,0:T(4,128)(2,1)} %fusion.7) | data formatting | bytes 1048576 | tf_op jit(solution)/shard_map/convert_element_type | solution.py:17
  38.3 0.0 reduce-scatter.4.cloned.1.call-update
  38.3 0.0 reduce-scatter.6.cloned.1.call-start
  38.4 22.4 %reduce-scatter.4.cloned.1.call-done = bf16[512,128]{0,1:T(8,128)(2,1)} async-done(((bf16[512,512]{0,1:T(8,128)(2,1)}), bf16[512,128]{0,1:T(8,128)(2,1)}) %reduce-scatter.4.cloned.1.call-update) | async-done | bytes 131088 | tf_op jit(solution)/shard_map/reduce_scatter | solution.py:16
  60.8 16.0 %all_gather.13 = bf16[512,512]{0,1:T(8,128)(2,1)S(1)} all-gather(bf16[512,128]{0,1:T(8,128)(2,1)} %reduce-scatter.4.cloned.1.call-done), channel_id=1, replica_groups=mesh['groups'=2,'row'=4,'col'=4] {'row'}, dimensions={1}, use_global_device_ids=true | all-gather | bytes 655360 | tf_op jit(solution)/shard_map/all_gather | solution.py:12
  76.8 0.3 copy.50
  77.1 0.8 gather_fusion
  77.9 0.0 copy-start.1
  77.9 0.5 bitcast_reduce_fusion
  78.4 1.0 copy.52
  79.4 0.0 reduce-scatter.6.cloned.1.call-update
  79.4 0.0 reduce-scatter.8.cloned.1.call-start
  79.5 0.0 copy-done.1
  79.5 0.1 copy.53
  79.6 19.9 %reduce-scatter.6.cloned.1.call-done = bf16[512,128]{0,1:T(8,128)(2,1)} async-done(((bf16[512,512]{0,1:T(8,128)(2,1)}), bf16[512,128]{0,1:T(8,128)(2,1)}) %reduce-scatter.6.cloned.1.call-update) | async-done | bytes 131088 | tf_op jit(solution)/shard_map/reduce_scatter | solution.py:57
  99.5 0.9 subtract_convert_fusion
  100.5 6.8 %all_gather.14 = bf16[512,512]{0,1:T(8,128)(2,1)S(1)} all-gather(bf16[512,128]{0,1:T(8,128)(2,1)S(1)} %subtract_convert_fusion), channel_id=1, replica_groups=mesh['groups'=2,'row'=4,'col'=4] {'col'}, dimensions={1}, use_global_device_ids=true | all-gather | bytes 655360 | tf_op jit(solution)/shard_map/all_gather | solution.py:8
  107.2 0.3 copy.54
  107.5 0.1 broadcast_in_dim.20
  107.7 0.4 convolution_bitcast_fusion
  108.1 2.2 %fusion.8 = bf16[512,4,128]{2,1,0:T(4,128)(2,1)S(1)} fusion(f32[512,8,128]{2,0,1:T(8,128)S(1)} %convolution_bitcast_fusion, s32[8]{0:T(128)S(1)} %min.12, pred[8]{0:T(512)(128)(4,1)S(1)} %ge.15), kind=kOutput, calls=%fused_computation.12 | convolution fusion | flops 25428032 | bytes 2621480 | tf_op jit(solution)/shard_map/psb,sj->pjb/dot_general | solution.py:47
  110.3 1.1 copy.69
  111.5 0.0 copy-start.2
  111.5 0.0 copy-start
  111.5 0.0 reduce-scatter.8.cloned.1.call-update
  111.5 4.5 %all-to-all-start.2 = ((bf16[1,4,2,6,128,128]{5,4,3,2,0,1:T(8,128)(2,1)}), bf16[1,4,2,6,128,128]{5,4,3,2,0,1:T(8,128)(2,1)}, u32[]{:S(2)}, u32[]{:S(2)}) async-start(bf16[1,4,2,6,128,128]{5,4,3,2,0,1:T(8,128)(2,1)} %bitcast.23), calls=%async_computation.5 | async-start | bytes 3145728 | tf_op jit(solution)/shard_map/all_to_all | solution.py:28
  116.0 0.0 copy-done.2
  116.0 0.6 fusion.32
  116.6 17.0 %reduce-scatter.8.cloned.1.call-done = bf16[512,128]{0,1:T(8,128)(2,1)} async-done(((bf16[512,512]{0,1:T(8,128)(2,1)}), bf16[512,128]{0,1:T(8,128)(2,1)}) %reduce-scatter.8.cloned.1.call-update) | async-done | bytes 131088 | tf_op jit(solution)/shard_map/reduce_scatter | solution.py:16
  133.6 0.0 copy-done
  133.6 2.3 %fusion.24 = bf16[512,128]{0,1:T(8,128)(2,1)S(1)} fusion(bf16[512,128]{0,1:T(8,128)(2,1)S(1)} %copy-done, bf16[512,128]{0,1:T(8,128)(2,1)} %reduce-scatter.8.cloned.1.call-done, f32[]{:T(128)} %bitcast.8, f32[]{:T(128)} %bitcast), kind=kLoop, calls=%fused_computation.28 | loop fusion | flops 524288 | bytes 393224 | tf_op jit(solution)/shard_map/convert_element_type | solution.py:63
  135.8 0.8 copy.61
  136.6 15.9 %all_gather.15 = bf16[512,512]{0,1:T(8,128)(2,1)S(1)} all-gather(bf16[512,128]{0,1:T(8,128)(2,1)S(1)} %fusion.24), channel_id=1, replica_groups=mesh['groups'=2,'row'=4,'col'=4] {'row'}, dimensions={1}, use_global_device_ids=true | all-gather | bytes 655360 | tf_op jit(solution)/shard_map/all_gather | solution.py:12
  152.4 0.3 copy.58
  152.7 0.8 gather_fusion.1
  153.5 0.6 fusion.11
  154.0 0.4 copy.65
  154.5 0.0 all-to-all-done.2
  154.5 3.5 %fusion = f32[8,1,6,1]{2,1,3,0:T(1,128)S(1)} fusion(bf16[8,128,128,1]{2,3,1,0:T(2,128)(2,1)S(1)} %copy.65, bf16[8,6,128,128]{3,2,1,0:T(8,128)(2,1)} %bitcast.24), kind=kOutput, calls=%fused_computation.3 | convolution fusion | flops 1572864 | bytes 1835200 | tf_op jit(solution)/shard_map/skab,sab->ks/dot_general | solution.py:75
  158.0 6.2 %psum.7 = f32[6,4]{0,1:T(4,128)} all-reduce(f32[6,4]{0,1:T(4,128)S(1)} %broadcast_multiply_fusion), channel_id=1, replica_groups=mesh['groups'=2,'row'=4,'col'=4] {'col'}, use_global_device_ids=true, to_apply=%region_5.7 | all-reduce | flops 24 | bytes 192 | tf_op jit(solution)/shard_map/psum | solution.py:79
  (7 shorter events, 0.1 us)
Async XLA Ops:
  8.5 12.2 %all-to-all-start = ((s32[1,4,2]{2,0,1:T(1,128)}), s32[1,4,2]{2,0,1:T(1,128)S(1)}, u32[]{:S(2)}, u32[]{:S(2)}) async-start(s32[1,4,2]{2,0,1:T(1,128)} %copy.44), calls=%async_computation | async-start | bytes 4096 | tf_op jit(solution)/shard_map/all_to_all | solution.py:29
  20.7 9.4 %all-to-all-start.1 = ((bf16[1,4,2,128,128]{4,3,2,0,1:T(8,128)(2,1)}), bf16[1,4,2,128,128]{4,3,2,0,1:T(8,128)(2,1)S(1)}, u32[]{:S(2)}, u32[]{:S(2)}) async-start(bf16[1,4,2,128,128]{4,3,2,0,1:T(8,128)(2,1)} %bitcast.77), calls=%async_computation.1 | async-start | bytes 524288 | tf_op jit(solution)/shard_map/all_to_all | solution.py:27
  24.2 36.6 %reduce-scatter.4.cloned.1.call-start = ((), (), s32[]{:S(2)}) async-start(), calls=%async_computation.6 | async-start | bytes 655360 | tf_op jit(solution)/shard_map/reduce_scatter | solution.py:16
  38.3 61.2 %reduce-scatter.6.cloned.1.call-start = ((), (), s32[]{:S(2)}) async-start(), calls=%async_computation.7 | async-start | bytes 655360 | tf_op jit(solution)/shard_map/reduce_scatter | solution.py:57
  77.9 1.6 copy-start.1
  79.4 54.1 %reduce-scatter.8.cloned.1.call-start = ((), (), s32[]{:S(2)}) async-start(), calls=%async_computation.8 | async-start | bytes 655360 | tf_op jit(solution)/shard_map/reduce_scatter | solution.py:16
  111.5 4.5 %copy-start.2 = (f32[2]{0:T(128)S(1)}, f32[2]{0:T(128)}, u32[]{:S(2)}) copy-start(f32[2]{0:T(128)} %param.11) | copy-start | bytes 28
  111.5 22.1 %copy-start = (bf16[512,128]{0,1:T(8,128)(2,1)S(1)}, bf16[512,128]{0,1:T(8,128)(2,1)}, u32[]{:S(2)}) copy-start(bf16[512,128]{0,1:T(8,128)(2,1)} %reduce-scatter.4.cloned.1.call-done) | copy-start | bytes 393220
  111.5 43.0 %all-to-all-start.2 = ((bf16[1,4,2,6,128,128]{5,4,3,2,0,1:T(8,128)(2,1)}), bf16[1,4,2,6,128,128]{5,4,3,2,0,1:T(8,128)(2,1)}, u32[]{:S(2)}, u32[]{:S(2)}) async-start(bf16[1,4,2,6,128,128]{5,4,3,2,0,1:T(8,128)(2,1)} %bitcast.23), calls=%async_computation.5 | async-start | bytes 3145728 | tf_op jit(solution)/shard_map/all_to_all | solution.py:28
Sparse Core Ops, SparseCore 0:
  38.4 22.3 reduce-scatter.3
  79.5 19.9 reduce-scatter.5
  111.6 21.9 reduce-scatter.7
where the time goes:
time: 171 us
  waiting for transfers between devices  65.1 us (38%)
  blocking collectives  52.8 us (31%)
  between operations  13.9 us (8%)
  local copies, waits for them, and re-layouts  12.4 us (7%)
  starting transfers between devices  12.3 us (7%)
  matrix products  11 us (6%)
  other arithmetic  3.3 us (2%)
    reduce_scatter x2, waiting for transfers between devices, down_sum(): lax.psum_scatter(partial_value.astype(jnp.bfloat16), 'row', scatter_dimen...  39.4 us
    all_gather x2, blocking collectives, along_col(): return lax.all_gather(panel, 'row', axis=1, tiled=True)  31.9 us
    reduce_scatter x1, waiting for transfers between devices, local(): lax.psum_scatter(partial_two.astype(jnp.bfloat16), 'col', scatter_dimensi...  19.9 us
    all_gather x2, blocking collectives, along_row(): return lax.all_gather(panel, 'col', axis=1, tiled=True)  14.7 us
    psum x1, blocking collectives, local(): stress = lax.psum(row_terms, 'col')  6.24 us
    all_to_all x1, waiting for transfers between devices, local(): lax.all_to_all(ham_blocks, 'col', split_axis=1, concat_axis=0, tiled=True)  5.73 us
    all_to_all x1, starting transfers between devices, local(): lax.all_to_all(strain_blocks, 'col', split_axis=1, concat_axis=0, tiled=T...  4.48 us
    all_to_all x1, starting transfers between devices, local(): lax.all_to_all(block_cols, 'col', split_axis=1, concat_axis=0, tiled=True)  4.24 us
  transfers between devices with their start and end apart: 6, of which 4 were waited for; matrix products, arithmetic and copies ran while one was open for 4% of the time, Pallas kernels for 0%

commit v1 on v0

--- a/solution.py
+++ b/solution.py
@@ -1,7 +1,298 @@
+import functools
+
 import jax
 import jax.numpy as jnp
 from jax import lax
+from jax.experimental import pallas as pl
+from jax.experimental.pallas import tpu as pltpu
 from jax.sharding import PartitionSpec as P
+
+MESH = pl.DeviceIdType.MESH
+
+
+def fused_kernel(
+    n_row,
+    probes_ref, ham_ref, strain_ref, cols_ref, coeffs_ref,
+    out_ref, stress_ref,
+    hbuf, pbuf, xbuf, cbuf, csm, sbuf, strain_buf, x0t, x1t, x2t, dsend, dmine,
+    hs, hr, ps, pr, xs, xr, cs, cr, das, dar, dbs, dbr, ss, sr, loc,
+):
+    n_col = 4
+    nb = n_row * n_col
+    grp = lax.axis_index("groups")
+    z = lax.axis_index("row")
+    c = lax.axis_index("col")
+    me = z * n_col + c
+    sib = c + 1 - 2 * (c % 2)
+    yc = (c + 2) % 4
+    ysib = sib + 2 - 4 * (sib // 2)
+    slots = hbuf.shape[1]
+    chunks = hr.shape[1]
+    per = slots // chunks
+    sub = xbuf.shape[1]
+    comps = strain_buf.shape[1]
+
+    def dev(row, col):
+        return (grp, row, col)
+
+    def others():
+        for d in range(1, nb):
+            k = (me + d) % nb
+            yield d, k
+
+    barrier = pltpu.get_barrier_semaphore()
+    for _, k in others():
+        pl.semaphore_signal(barrier, inc=1, device_id=dev(k // n_col, k % n_col), device_id_type=MESH)
+    strain_copy = pltpu.make_async_copy(strain_ref, strain_buf, loc.at[0])
+    strain_copy.start()
+    own_ham = pltpu.make_async_copy(ham_ref, hbuf.at[me], loc.at[1])
+    own_ham.start()
+    pbuf[me] = probes_ref[...]
+    cbuf[me] = cols_ref[...]
+    xbuf[me] = probes_ref[pl.ds(pl.multiple_of(me * sub, sub), sub), :]
+    pl.semaphore_wait(barrier, nb - 1)
+
+    waits = []
+
+    def remote(src, dst, send, recv, target):
+        return pltpu.make_async_remote_copy(
+            src_ref=src, dst_ref=dst, send_sem=send, recv_sem=recv, device_id=target, device_id_type=MESH
+        )
+
+    def launch(copy, pred=None):
+        if pred is None:
+            copy.start()
+        else:
+            @pl.when(pred)
+            def _():
+                copy.start()
+        waits.append((copy, pred))
+
+    def small(src_of, dst, send, recv, place=lambda k: (k // n_col, k % n_col)):
+        for d, k in others():
+            launch(remote(src_of(k), dst, send.at[d], recv.at[me], dev(*place(k))))
+
+    def small_wait(dst, send, recv):
+        for d, k in others():
+            remote(dst.at[k], dst.at[k], send.at[d], recv.at[k], dev(z, sib)).wait_recv()
+
+    small(lambda k: cbuf.at[me], cbuf.at[me], cs, cr)
+    small(lambda k: probes_ref.at[pl.ds(pl.multiple_of(k * sub, sub), sub)], xbuf.at[me], xs, xr)
+
+    def ham_piece(org, m):
+        return hbuf.at[org, pl.ds(m * per, per)]
+
+    def ham_send(org, m, way, target, pred=None):
+        src = ham_ref.at[pl.ds(m * per, per)] if org is me else ham_piece(org, m)
+        launch(remote(src, ham_piece(org, m), hs.at[org, m, way], hr.at[org, m], target), pred)
+
+    def ham_recv(org, m):
+        remote(ham_piece(org, m), ham_piece(org, m), hs.at[org, m, 0], hr.at[org, m], dev(z, sib)).wait_recv()
+
+    def probe_send(org, m, way, target, pred=None):
+        launch(remote(pbuf.at[org], pbuf.at[org], ps.at[org, way], pr.at[org], target), pred)
+
+    def probe_recv(org, m):
+        remote(pbuf.at[org], pbuf.at[org], ps.at[org, 0], pr.at[org], dev(z, sib)).wait_recv()
+
+    up, down = z + 1, z - 1
+    has_up, has_down = z < n_row - 1, z > 0
+
+    def first(send, pieces):
+        for m in range(pieces):
+            send(me, m, 0, dev(jnp.minimum(up, n_row - 1), c), has_up)
+            send(me, m, 1, dev(jnp.maximum(down, 0), c), has_down)
+            send(me, m, 2, dev(z, yc))
+            send(me, m, 3, dev(z, sib))
+
+    def wave(d, send, recv, pieces):
+        for m in range(pieces):
+            if d < n_row:
+                for sgn in (-1, 1):
+                    zo = z + sgn * d
+                    ok = zo >= 0 if sgn < 0 else zo <= n_row - 1
+                    org = jnp.clip(zo, 0, n_row - 1) * n_col + c
+
+                    @pl.when(ok)
+                    def _():
+                        recv(org, m)
+                    if d < n_row - 1:
+                        if sgn < 0:
+                            send(org, m, 0, dev(jnp.minimum(up, n_row - 1), c), jnp.logical_and(ok, has_up))
+                        else:
+                            send(org, m, 1, dev(jnp.maximum(down, 0), c), jnp.logical_and(ok, has_down))
+                    send(org, m, 2, dev(z, yc), ok)
+                    send(org, m, 3, dev(z, sib), ok)
+            for sgn in (-1, 1) if d > 1 else (1,):
+                zo = z + sgn * (d - 1)
+                ok = zo >= 0 if sgn < 0 else zo <= n_row - 1
+                org = jnp.clip(zo, 0, n_row - 1) * n_col + yc
+
+                @pl.when(ok)
+                def _():
+                    recv(org, m)
+                send(org, m, 3, dev(z, sib), ok)
+
+    def last(recv, pieces):
+        for row in range(n_row):
+            for m in range(pieces):
+                recv(row * n_col + sib, m)
+                recv(row * n_col + ysib, m)
+
+    first(ham_send, chunks)
+    first(probe_send, 1)
+
+    small_wait(cbuf, cs, cr)
+    cols_copy = pltpu.make_async_copy(cbuf, csm, loc.at[2])
+    cols_copy.start()
+    small_wait(xbuf, xs, xr)
+    for j in range(nb):
+        x0t[j] = xbuf[j].astype(jnp.float32).T.astype(jnp.bfloat16)
+    cols_copy.wait()
+
+    for d in range(1, n_row + 1):
+        wave(d, ham_send, ham_recv, chunks)
+    own_ham.wait()
+    last(ham_recv, chunks)
+
+    groups = csm.shape[1]
+    cap = csm.shape[2]
+
+    def col_of(i, s):
+        return jnp.clip(csm[i, s // cap, s % cap], 0, nb - 1)
+
+    def product(x_ref, i):
+        weights = jnp.concatenate([x_ref[col_of(i, s)] for s in range(slots)], axis=0)
+        rows = jnp.concatenate([hbuf[i, s] for s in range(slots)], axis=1)
+        return jnp.dot(rows, weights, preferred_element_type=jnp.float32)
+
+    def one(i, carry):
+        x1t[i] = product(x0t, i).astype(jnp.bfloat16)
+        return carry
+
+    def two(i, carry):
+        x2t[i] = (2.0 * product(x1t, i) - x0t[i].astype(jnp.float32)).astype(jnp.bfloat16)
+        return carry
+
+    def three(i, carry):
+        prior = x1t[i].astype(jnp.float32)
+        third = 2.0 * product(x2t, i) - prior
+        dense = coeffs_ref[0] * prior + coeffs_ref[1] * third
+        dsend[i] = dense.T.astype(jnp.bfloat16)
+        return carry
+
+    wave(1, probe_send, probe_recv, 1)
+    lax.fori_loop(0, nb, one, 0)
+    wave(2, probe_send, probe_recv, 1)
+    lax.fori_loop(0, nb, two, 0)
+    wave(3, probe_send, probe_recv, 1)
+    lax.fori_loop(0, nb, three, 0)
+
+    small(lambda k: dsend.at[k], dmine.at[me], das, dar)
+    dmine[me] = dsend[me]
+
+    def swap(k):
+        return (k % n_col, k // n_col)
+
+    mine_out = c * n_row + z
+    for d in range(1, nb):
+        k = (mine_out + d) % nb
+        row, col = k % n_row, k // n_row
+        launch(remote(dsend.at[k], out_ref.at[me], dbs.at[d], dbr.at[me], dev(row, col)))
+    out_ref[me] = dsend[mine_out]
+    for d in range(4, n_row + 1):
+        wave(d, probe_send, probe_recv, 1)
+    last(probe_recv, 1)
+
+    small_wait(dmine, das, dar)
+    strain_copy.wait()
+    dens = dmine[...].reshape(nb * sub, dmine.shape[2])
+    dens_t = dens.astype(jnp.float32).T.astype(jnp.bfloat16)
+    lane = lax.broadcasted_iota(jnp.int32, (comps, 128), 1)
+    part = jnp.zeros((comps, 128), jnp.float32)
+    for s in range(slots):
+        col = col_of(me, s)
+        tile = jnp.dot(dens_t, pbuf[col], preferred_element_type=jnp.float32)
+        sums = jnp.concatenate(
+            [
+                jnp.sum(strain_buf[s, k].astype(jnp.float32) * tile, axis=0, keepdims=True)
+                for k in range(comps)
+            ],
+            axis=0,
+        )
+        part = part + jnp.where(lane == col, jnp.sum(sums, axis=1, keepdims=True), 0.0)
+    sbuf[me] = jnp.concatenate([part, jnp.zeros((sbuf.shape[1] - comps, 128), jnp.float32)], axis=0)
+    small(lambda k: sbuf.at[me], sbuf.at[me], ss, sr)
+    small_wait(out_ref, dbs, dbr)
+    small_wait(sbuf, ss, sr)
+    total = jnp.sum(sbuf[...], axis=0) * (1.0 / (nb * sub))
+    picked = total[:comps, 0:n_col]
+    for row in range(1, n_row):
+        picked = jnp.where(z == row, total[:comps, row * n_col:(row + 1) * n_col], picked)
+    stress_ref[...] = picked
+
+    for copy, pred in waits:
+        if pred is None:
+            copy.wait_send()
+        else:
+            @pl.when(pred)
+            def _(copy=copy):
+                copy.wait_send()
+
+
+def fused_local(n_row, probes, ham_blocks, strain_blocks, block_cols, odd_coeffs):
+    n_col = 4
+    nb = n_row * n_col
+    probe_count, block = probes.shape
+    _, groups, cap, comps = strain_blocks.shape[:4]
+    slots = groups * cap
+    sub = probe_count // nb
+    chunks = 2
+    bf16, f32 = jnp.bfloat16, jnp.float32
+    dma = pltpu.SemaphoreType.DMA
+    vmem = pl.BlockSpec(memory_space=pltpu.VMEM)
+    hbm = pl.BlockSpec(memory_space=pl.ANY)
+    density, stress = pl.pallas_call(
+        functools.partial(fused_kernel, n_row),
+        out_shape=(
+            jax.ShapeDtypeStruct((nb, sub, block), bf16),
+            jax.ShapeDtypeStruct((comps, n_col), f32),
+        ),
+        in_specs=[vmem, hbm, hbm, vmem, pl.BlockSpec(memory_space=pltpu.SMEM)],
+        out_specs=(vmem, vmem),
+        scratch_shapes=[
+            pltpu.VMEM((nb, slots, block, block), bf16),
+            pltpu.VMEM((nb, probe_count, block), bf16),
+            pltpu.VMEM((nb, sub, block), bf16),
+            pltpu.VMEM((nb, groups, cap), jnp.int32),
+            pltpu.SMEM((nb, groups, cap), jnp.int32),
+            pltpu.VMEM((nb, 8, 128), f32),
+            pltpu.VMEM((slots, comps, block, block), bf16),
+            pltpu.VMEM((nb, block, sub), bf16),
+            pltpu.VMEM((nb, block, sub), bf16),
+            pltpu.VMEM((nb, block, sub), bf16),
+            pltpu.VMEM((nb, sub, block), bf16),
+            pltpu.VMEM((nb, sub, block), bf16),
+            dma((nb, chunks, 4)), dma((nb, chunks)),
+            dma((nb, 4)), dma((nb,)),
+            dma((nb,)), dma((nb,)),
+            dma((nb,)), dma((nb,)),
+            dma((nb,)), dma((nb,)),
+            dma((nb,)), dma((nb,)),
+            dma((nb,)), dma((nb,)),
+            dma((3,)),
+        ],
+        compiler_params=pltpu.CompilerParams(
+            collective_id=0, has_side_effects=True, vmem_limit_bytes=40 * 1024 * 1024
+        ),
+    )(
+        probes,
+        ham_blocks.reshape(slots, block, block),
+        strain_blocks.reshape(slots, comps, block, block),
+        block_cols.reshape(groups, cap),
+        odd_coeffs,
+    )
+    return density.reshape(probe_count, block), stress
 
 
 def along_row(panel):
@@ -88,8 +379,19 @@
         P(("groups", "row", "col"), None, None),
         P(),
     )
+    n_row, n_col = mesh.shape["row"], mesh.shape["col"]
+
+    def pick(*args):
+        probes, ham_blocks = args[0], args[1]
+        one_block = probes.shape[1] == ham_blocks.shape[-1] and ham_blocks.shape[0] == 1
+        held = n_row * n_col * (2 * ham_blocks.size + 2 * probes.size)
+        whole_rows = probes.shape[0] % (16 * n_row * n_col) == 0
+        if n_row == 4 and n_col == 4 and one_block and whole_rows and held <= 16 * 1024 * 1024:
+            return fused_local(n_row, *args)
+        return local(*args)
+
     return jax.shard_map(
-        local,
+        pick,
         mesh=mesh,
         in_specs=placed,
         out_specs=(P("groups", ("col", "row")), P("groups", "row")),

time: 171 us -> 73.7 us (0.43)
  Pallas kernels: 0 us -> 66.9 us
  waiting for transfers between devices: 65.1 us -> 0 us
  blocking collectives: 52.8 us -> 0 us
  between operations: 13.9 us -> 0.64 us
  starting transfers between devices: 12.3 us -> 0 us
  matrix products: 11 us -> 0 us
  local copies, waits for them, and re-layouts: 12.4 us -> 6 us
  other arithmetic: 3.3 us -> 0 us
    pallas_call x0 -> x1, Pallas kernels: none -> 66.9 us  [fused_local(): pl.pallas_call(functools.partial(fused_kernel, n_row), out_shape=(jax.Sha...]
    reduce_scatter x3 -> x0, waiting for transfers between devices: 59.3 us -> none  [the longest x2 39.4 us: down_sum(): lax.psum_scatter(partial_value.astype(jnp.bfloat16), 'row', scatter_dimen...]
    all_gather x4 -> x0, blocking collectives: 46.5 us -> none  [the longest x2 31.9 us: along_col(): return lax.all_gather(panel, 'row', axis=1, tiled=True)]
    all_to_all x3 -> x0, starting transfers between devices: 12.1 us -> none  [the longest x1 4.48 us: local(): lax.all_to_all(strain_blocks, 'col', split_axis=1, concat_axis=0, tiled=T...]
    dot_general x7 -> x0, matrix products: 11 us -> none  [the longest x2 4.15 us: backward(): jnp.einsum('psb,sj->pjb', contrib, placement, precision=lax.Precision.HIG...]
    psum x1 -> x0, blocking collectives: 6.24 us -> none  [local(): stress = lax.psum(row_terms, 'col')]
    all_to_all x3 -> x0, waiting for transfers between devices: 5.74 us -> none  [the longest x1 5.73 us: local(): lax.all_to_all(ham_blocks, 'col', split_axis=1, concat_axis=0, tiled=True)]
    convert_element_type x4 -> x0, local copies, waits for them, and re-layouts: 4.64 us -> none  [the longest x2 3.24 us: down_sum(): partial_value.astype(jnp.bfloat16)]
  transfers between devices with their start and end apart: 6 -> 0, of which waited for: 4 -> 0; matrix products, arithmetic and copies ran while one was open for 4% -> 0% of each run, Pallas kernels for 0% -> 0%
where the time goes in v1:
time: 73.7 us; the launch traced here: 73.5 us
  Pallas kernels  66.9 us (91%)
  local copies, waits for them, and re-layouts  6 us (8%)
    pallas_call x1, Pallas kernels, fused_local(): pl.pallas_call(functools.partial(fused_kernel, n_row), out_shape=(jax.Sha...  66.9 us
    unnamed x10, local copies, waits for them, and re-layouts  5.23 us

profile of v1, /device:TPU:0, one launch (start us, length us, event | category | flops | bytes accessed | tf_op | source)
XLA Modules:
  0.0 73.5 jit_solution(7025464722519422023)
XLA Ops:
  0.6 0.8 %copy.7.cols_ref = s32[4,2]{1,0:T(4,128)S(1)} copy(s32[4,2]{0,1:T(2,128)} %bitcast.7) | data formatting | bytes 64 | tf_op jit(solution)/shard_map/reshape | solution.py:292
  1.4 0.0 copy-start
  1.4 1.4 %copy-done = bf16[1,4,2,6,128,128]{5,4,3,2,1,0:T(8,128)(2,1)S(1)} copy-done((bf16[1,4,2,6,128,128]{5,4,3,2,1,0:T(8,128)(2,1)S(1)}, bf16[1,4,2,6,128,128]{5,4,3,2,1,0:T(8,128)(2,1)}, u32[]{:S(2)}) %copy-start) | copy-done | bytes 1572888
  2.8 0.0 copy-start.1
  2.8 0.9 %copy-done.1 = bf16[1,4,2,128,128]{4,3,2,1,0:T(8,128)(2,1)S(1)} copy-done((bf16[1,4,2,128,128]{4,3,2,1,0:T(8,128)(2,1)S(1)}, bf16[1,4,2,128,128]{4,3,2,1,0:T(8,128)(2,1)}, u32[]{:S(2)}) %copy-start.1) | copy-done | bytes 262168
  3.8 0.0 copy-start.2
  3.8 0.9 %copy-done.2 = bf16[512,128]{1,0:T(8,128)(2,1)S(1)} copy-done((bf16[512,128]{1,0:T(8,128)(2,1)S(1)}, bf16[512,128]{1,0:T(8,128)(2,1)}, u32[]{:S(2)}) %copy-start.2) | copy-done | bytes 131096
  4.7 0.0 copy-start.3
  4.7 0.7 copy-done.3
  5.3 66.9 %shard_map.68 = (bf16[16,32,128]{2,1,0:T(8,128)(2,1)S(1)}, f32[6,4]{1,0:T(8,128)S(1)}) custom-call(bf16[512,128]{1,0:T(8,128)(2,1)S(1)} %copy-done.2, bf16[8,128,128]{2,1,0:T(8,128)(2,1)S(1)} %bitcast.5, bf16[8,6,128,128]{3,2,1,0:T(8,128)(2,1)S(1)} %bitcast.4, s32[4,2]{1,0:T(4,128)S(1)} %copy.7.cols_ref, f32[2]{0:T(128)S(1)} %copy-done.3), custom_call_target="tpu_custom_call" | custom-call | tf_op jit(solution)/shard_map/pallas_call | solution.py:255
  72.2 0.7 copy.8
  72.9 0.7 copy.10
Async XLA Ops:
  1.4 1.4 %copy-start = (bf16[1,4,2,6,128,128]{5,4,3,2,1,0:T(8,128)(2,1)S(1)}, bf16[1,4,2,6,128,128]{5,4,3,2,1,0:T(8,128)(2,1)}, u32[]{:S(2)}) copy-start(bf16[1,4,2,6,128,128]{5,4,3,2,1,0:T(8,128)(2,1)} %param.7) | copy-start | bytes 4718596
  2.8 0.9 %copy-start.1 = (bf16[1,4,2,128,128]{4,3,2,1,0:T(8,128)(2,1)S(1)}, bf16[1,4,2,128,128]{4,3,2,1,0:T(8,128)(2,1)}, u32[]{:S(2)}) copy-start(bf16[1,4,2,128,128]{4,3,2,1,0:T(8,128)(2,1)} %param.6) | copy-start | bytes 786436
  3.8 0.9 %copy-start.2 = (bf16[512,128]{1,0:T(8,128)(2,1)S(1)}, bf16[512,128]{1,0:T(8,128)(2,1)}, u32[]{:S(2)}) copy-start(bf16[512,128]{1,0:T(8,128)(2,1)} %probes_ref.1) | copy-start | bytes 393220
  4.7 0.7 copy-start.3

commit v2 on v1

--- a/solution.py
+++ b/solution.py
@@ -14,7 +14,7 @@
     n_row,
     probes_ref, ham_ref, strain_ref, cols_ref, coeffs_ref,
     out_ref, stress_ref,
-    hbuf, pbuf, xbuf, cbuf, csm, sbuf, strain_buf, x0t, x1t, x2t, dsend, dmine,
+    hbuf, pbuf, xbuf, cbuf, csm, coeffs, sbuf, strain_buf, x0t, x1t, x2t, dsend, dmine,
     hs, hr, ps, pr, xs, xr, cs, cr, das, dar, dbs, dbr, ss, sr, loc,
 ):
     n_col = 4
@@ -26,9 +26,9 @@
     sib = c + 1 - 2 * (c % 2)
     yc = (c + 2) % 4
     ysib = sib + 2 - 4 * (sib // 2)
-    slots = hbuf.shape[1]
+    groups, cap = hbuf.shape[1:3]
+    slots = groups * cap
     chunks = hr.shape[1]
-    per = slots // chunks
     sub = xbuf.shape[1]
     comps = strain_buf.shape[1]
 
@@ -43,13 +43,22 @@
     barrier = pltpu.get_barrier_semaphore()
     for _, k in others():
         pl.semaphore_signal(barrier, inc=1, device_id=dev(k // n_col, k % n_col), device_id_type=MESH)
-    strain_copy = pltpu.make_async_copy(strain_ref, strain_buf, loc.at[0])
-    strain_copy.start()
-    own_ham = pltpu.make_async_copy(ham_ref, hbuf.at[me], loc.at[1])
-    own_ham.start()
-    pbuf[me] = probes_ref[...]
-    cbuf[me] = cols_ref[...]
-    xbuf[me] = probes_ref[pl.ds(pl.multiple_of(me * sub, sub), sub), :]
+    own = pl.ds(pl.multiple_of(me * sub, sub), sub)
+    local_copies = [
+        pltpu.make_async_copy(src, dst, loc.at[n])
+        for n, (src, dst) in enumerate(
+            [
+                (cols_ref, cbuf.at[me]),
+                (probes_ref.at[own], xbuf.at[me]),
+                (coeffs_ref, coeffs),
+                (ham_ref, hbuf.at[me]),
+                (probes_ref, pbuf.at[me]),
+                (strain_ref, strain_buf),
+            ]
+        )
+    ]
+    for copy in local_copies:
+        copy.start()
     pl.semaphore_wait(barrier, nb - 1)
 
     waits = []
@@ -76,21 +85,40 @@
         for d, k in others():
             remote(dst.at[k], dst.at[k], send.at[d], recv.at[k], dev(z, sib)).wait_recv()
 
-    small(lambda k: cbuf.at[me], cbuf.at[me], cs, cr)
+    small(lambda k: cols_ref, cbuf.at[me], cs, cr)
     small(lambda k: probes_ref.at[pl.ds(pl.multiple_of(k * sub, sub), sub)], xbuf.at[me], xs, xr)
 
+    def sends_third(row):
+        return jnp.logical_or(row == 0, row == n_row - 1)
+
     def ham_piece(org, m):
-        return hbuf.at[org, pl.ds(m * per, per)]
+        return hbuf.at[org, (org // n_col + m) % groups]
+
+    def with_third(org, m, pred):
+        if m < 2:
+            return pred
+        third = sends_third(org // n_col)
+        return third if pred is None else jnp.logical_and(pred, third)
 
     def ham_send(org, m, way, target, pred=None):
-        src = ham_ref.at[pl.ds(m * per, per)] if org is me else ham_piece(org, m)
-        launch(remote(src, ham_piece(org, m), hs.at[org, m, way], hr.at[org, m], target), pred)
+        src = ham_ref.at[(z + m) % groups] if org is me else ham_piece(org, m)
+        launch(
+            remote(src, ham_piece(org, m), hs.at[org, m, way], hr.at[org, m], target),
+            with_third(org, m, pred),
+        )
 
     def ham_recv(org, m):
-        remote(ham_piece(org, m), ham_piece(org, m), hs.at[org, m, 0], hr.at[org, m], dev(z, sib)).wait_recv()
+        copy = remote(ham_piece(org, m), ham_piece(org, m), hs.at[org, m, 0], hr.at[org, m], dev(z, sib))
+        if m < 2:
+            copy.wait_recv()
+        else:
+            @pl.when(sends_third(org // n_col))
+            def _():
+                copy.wait_recv()
 
     def probe_send(org, m, way, target, pred=None):
-        launch(remote(pbuf.at[org], pbuf.at[org], ps.at[org, way], pr.at[org], target), pred)
+        src = probes_ref if org is me else pbuf.at[org]
+        launch(remote(src, pbuf.at[org], ps.at[org, way], pr.at[org], target), pred)
 
     def probe_recv(org, m):
         remote(pbuf.at[org], pbuf.at[org], ps.at[org, 0], pr.at[org], dev(z, sib)).wait_recv()
@@ -143,27 +171,49 @@
     first(probe_send, 1)
 
     small_wait(cbuf, cs, cr)
-    cols_copy = pltpu.make_async_copy(cbuf, csm, loc.at[2])
+    local_copies[0].wait()
+    cols_copy = pltpu.make_async_copy(cbuf, csm, loc.at[6])
     cols_copy.start()
     small_wait(xbuf, xs, xr)
+    local_copies[1].wait()
     for j in range(nb):
         x0t[j] = xbuf[j].astype(jnp.float32).T.astype(jnp.bfloat16)
     cols_copy.wait()
+    local_copies[2].wait()
 
     for d in range(1, n_row + 1):
         wave(d, ham_send, ham_recv, chunks)
-    own_ham.wait()
+    local_copies[3].wait()
     last(ham_recv, chunks)
 
-    groups = csm.shape[1]
-    cap = csm.shape[2]
+    wave(1, probe_send, probe_recv, 1)
 
     def col_of(i, s):
-        return jnp.clip(csm[i, s // cap, s % cap], 0, nb - 1)
+        return jnp.clip(csm[i, s % cap, s // cap], 0, nb - 1)
+
+    def mirror(a, g):
+        def one_row(w, carry):
+            i = a * n_col + w
+            for s in range(cap):
+                raw = csm[i, s, g]
+                j = jnp.clip(raw, 0, nb - 1)
+                place = jnp.int32(0)
+                for t in range(1, cap):
+                    place = jnp.where(csm[j, t, a] == i, t, place)
+                block = hbuf[j, a, place].T
+                hbuf[i, g, s] = jnp.where(raw >= 0, block, jnp.zeros_like(block))
+            return carry
+
+        lax.fori_loop(0, n_col, one_row, 0, unroll=True)
+
+    for g in range(groups):
+        mirror((g + 1) % groups, g)
+        if g in (0, n_row - 1):
+            mirror((g + 2) % groups, g)
 
     def product(x_ref, i):
         weights = jnp.concatenate([x_ref[col_of(i, s)] for s in range(slots)], axis=0)
-        rows = jnp.concatenate([hbuf[i, s] for s in range(slots)], axis=1)
+        rows = jnp.concatenate([hbuf[i, s // cap, s % cap] for s in range(slots)], axis=1)
         return jnp.dot(rows, weights, preferred_element_type=jnp.float32)
 
     def one(i, carry):
@@ -174,38 +224,38 @@
         x2t[i] = (2.0 * product(x1t, i) - x0t[i].astype(jnp.float32)).astype(jnp.bfloat16)
         return carry
 
-    def three(i, carry):
+    mine_out = c * n_row + z
+
+    def density_copies(k):
+        return (
+            (k != me, remote(dsend.at[k], dmine.at[me], das.at[k], dar.at[me], dev(k // n_col, k % n_col))),
+            (k != mine_out, remote(dsend.at[k], out_ref.at[me], dbs.at[k], dbr.at[me], dev(k % n_row, k // n_row))),
+        )
+
+    def three(t, carry):
+        i = (me + 1 + t) % nb
         prior = x1t[i].astype(jnp.float32)
         third = 2.0 * product(x2t, i) - prior
-        dense = coeffs_ref[0] * prior + coeffs_ref[1] * third
+        dense = coeffs[0] * prior + coeffs[1] * third
         dsend[i] = dense.T.astype(jnp.bfloat16)
+        for pred, copy in density_copies(i):
+            pl.when(pred)(copy.start)
         return carry
 
-    wave(1, probe_send, probe_recv, 1)
-    lax.fori_loop(0, nb, one, 0)
+    lax.fori_loop(0, nb, one, 0, unroll=2)
     wave(2, probe_send, probe_recv, 1)
-    lax.fori_loop(0, nb, two, 0)
+    lax.fori_loop(0, nb, two, 0, unroll=2)
     wave(3, probe_send, probe_recv, 1)
     lax.fori_loop(0, nb, three, 0)
-
-    small(lambda k: dsend.at[k], dmine.at[me], das, dar)
     dmine[me] = dsend[me]
-
-    def swap(k):
-        return (k % n_col, k // n_col)
-
-    mine_out = c * n_row + z
-    for d in range(1, nb):
-        k = (mine_out + d) % nb
-        row, col = k % n_row, k // n_row
-        launch(remote(dsend.at[k], out_ref.at[me], dbs.at[d], dbr.at[me], dev(row, col)))
     out_ref[me] = dsend[mine_out]
     for d in range(4, n_row + 1):
         wave(d, probe_send, probe_recv, 1)
     last(probe_recv, 1)
 
     small_wait(dmine, das, dar)
-    strain_copy.wait()
+    local_copies[4].wait()
+    local_copies[5].wait()
     dens = dmine[...].reshape(nb * sub, dmine.shape[2])
     dens_t = dens.astype(jnp.float32).T.astype(jnp.bfloat16)
     lane = lax.broadcasted_iota(jnp.int32, (comps, 128), 1)
@@ -223,6 +273,16 @@
         part = part + jnp.where(lane == col, jnp.sum(sums, axis=1, keepdims=True), 0.0)
     sbuf[me] = jnp.concatenate([part, jnp.zeros((sbuf.shape[1] - comps, 128), jnp.float32)], axis=0)
     small(lambda k: sbuf.at[me], sbuf.at[me], ss, sr)
+    for k in range(nb):
+        for pred, copy in density_copies(k):
+            pl.when(pred)(copy.wait_send)
+    for copy, pred in waits:
+        if pred is None:
+            copy.wait_send()
+        else:
+            @pl.when(pred)
+            def _(copy=copy):
+                copy.wait_send()
     small_wait(out_ref, dbs, dbr)
     small_wait(sbuf, ss, sr)
     total = jnp.sum(sbuf[...], axis=0) * (1.0 / (nb * sub))
@@ -231,14 +291,6 @@
         picked = jnp.where(z == row, total[:comps, row * n_col:(row + 1) * n_col], picked)
     stress_ref[...] = picked
 
-    for copy, pred in waits:
-        if pred is None:
-            copy.wait_send()
-        else:
-            @pl.when(pred)
-            def _(copy=copy):
-                copy.wait_send()
-
 
 def fused_local(n_row, probes, ham_blocks, strain_blocks, block_cols, odd_coeffs):
     n_col = 4
@@ -247,25 +299,26 @@
     _, groups, cap, comps = strain_blocks.shape[:4]
     slots = groups * cap
     sub = probe_count // nb
-    chunks = 2
+    chunks = 3
     bf16, f32 = jnp.bfloat16, jnp.float32
     dma = pltpu.SemaphoreType.DMA
     vmem = pl.BlockSpec(memory_space=pltpu.VMEM)
-    hbm = pl.BlockSpec(memory_space=pl.ANY)
+    hbm = pl.BlockSpec(memory_space=pltpu.HBM)
     density, stress = pl.pallas_call(
         functools.partial(fused_kernel, n_row),
         out_shape=(
             jax.ShapeDtypeStruct((nb, sub, block), bf16),
             jax.ShapeDtypeStruct((comps, n_col), f32),
         ),
-        in_specs=[vmem, hbm, hbm, vmem, pl.BlockSpec(memory_space=pltpu.SMEM)],
+        in_specs=[hbm] * 5,
         out_specs=(vmem, vmem),
         scratch_shapes=[
-            pltpu.VMEM((nb, slots, block, block), bf16),
+            pltpu.VMEM((nb, groups, cap, block, block), bf16),
             pltpu.VMEM((nb, probe_count, block), bf16),
             pltpu.VMEM((nb, sub, block), bf16),
-            pltpu.VMEM((nb, groups, cap), jnp.int32),
-            pltpu.SMEM((nb, groups, cap), jnp.int32),
+            pltpu.VMEM((nb, cap, groups), jnp.int32),
+            pltpu.SMEM((nb, cap, groups), jnp.int32),
+            pltpu.SMEM((2,), f32),
             pltpu.VMEM((nb, 8, 128), f32),
             pltpu.VMEM((slots, comps, block, block), bf16),
             pltpu.VMEM((nb, block, sub), bf16),
@@ -280,16 +333,16 @@
             dma((nb,)), dma((nb,)),
             dma((nb,)), dma((nb,)),
             dma((nb,)), dma((nb,)),
-            dma((3,)),
+            dma((7,)),
         ],
         compiler_params=pltpu.CompilerParams(
             collective_id=0, has_side_effects=True, vmem_limit_bytes=40 * 1024 * 1024
         ),
     )(
         probes,
-        ham_blocks.reshape(slots, block, block),
+        ham_blocks.reshape(groups, cap, block, block),
         strain_blocks.reshape(slots, comps, block, block),
-        block_cols.reshape(groups, cap),
+        block_cols.reshape(groups, cap).T,
         odd_coeffs,
     )
     return density.reshape(probe_count, block), stress

time: 73.7 us -> 62.3 us (0.85)
  Pallas kernels: 66.9 us -> 55.6 us
    pallas_call x1, Pallas kernels: 66.9 us -> 55.6 us  [fused_local(): pl.pallas_call(functools.partial(fused_kernel, n_row), out_shape=(jax.Sha...]
    reshape x1 -> x0, local copies, waits for them, and re-layouts: 0.77 us -> none  [fused_local(): block_cols.reshape(groups, cap)]
    unnamed x10 -> x12, local copies, waits for them, and re-layouts: 5.23 us -> 5.91 us
where the time goes in v2:
time: 62.3 us; the launch traced here: 62.1 us
  Pallas kernels  55.6 us (89%)
  local copies, waits for them, and re-layouts  5.91 us (9%)
  between operations  0.65 us (1%)
    pallas_call x1, Pallas kernels, fused_local(): pl.pallas_call(functools.partial(fused_kernel, n_row), out_shape=(jax.Sha...  55.6 us
    unnamed x12, local copies, waits for them, and re-layouts  5.91 us

profile of v2, /device:TPU:0, one launch (start us, length us, event | category | flops | bytes accessed | tf_op | source)
XLA Modules:
  0.0 62.1 jit_solution(15180032454812251765)
XLA Ops:
  0.6 0.0 copy-start
  0.6 1.4 %copy-done = bf16[1,4,2,6,128,128]{5,4,3,2,1,0:T(8,128)(2,1)S(1)} copy-done((bf16[1,4,2,6,128,128]{5,4,3,2,1,0:T(8,128)(2,1)S(1)}, bf16[1,4,2,6,128,128]{5,4,3,2,1,0:T(8,128)(2,1)}, u32[]{:S(2)}) %copy-start) | copy-done | bytes 1572888
  2.0 0.0 copy-start.1
  2.0 0.9 %copy-done.1 = bf16[1,4,2,128,128]{4,3,2,1,0:T(8,128)(2,1)S(1)} copy-done((bf16[1,4,2,128,128]{4,3,2,1,0:T(8,128)(2,1)S(1)}, bf16[1,4,2,128,128]{4,3,2,1,0:T(8,128)(2,1)}, u32[]{:S(2)}) %copy-start.1) | copy-done | bytes 262168
  3.0 0.0 copy-start.2
  3.0 0.9 %copy-done.2 = bf16[512,128]{1,0:T(8,128)(2,1)S(1)} copy-done((bf16[512,128]{1,0:T(8,128)(2,1)S(1)}, bf16[512,128]{1,0:T(8,128)(2,1)}, u32[]{:S(2)}) %copy-start.2) | copy-done | bytes 131096
  3.9 0.0 copy-start.3
  3.9 0.7 %copy-done.3 = s32[1,4,2]{1,2,0:T(2,128)S(1)} copy-done((s32[1,4,2]{1,2,0:T(2,128)S(1)}, s32[1,4,2]{1,2,0:T(2,128)}, u32[]{:S(2)}) %copy-start.3) | copy-done | bytes 56
  4.6 0.0 copy-start.4
  4.6 0.7 %copy-done.4 = f32[2]{0:T(128)S(1)} copy-done((f32[2]{0:T(128)S(1)}, f32[2]{0:T(128)}, u32[]{:S(2)}) %copy-start.4) | copy-done | bytes 32
  5.2 55.6 %shard_map.68 = (bf16[16,32,128]{2,1,0:T(8,128)(2,1)S(1)}, f32[6,4]{1,0:T(8,128)S(1)}) custom-call(bf16[512,128]{1,0:T(8,128)(2,1)S(1)} %copy-done.2, bf16[4,2,128,128]{3,2,1,0:T(8,128)(2,1)S(1)} %bitcast.7, bf16[8,6,128,128]{3,2,1,0:T(8,128)(2,1)S(1)} %bitcast.6, s32[2,4]{1,0:T(2,128)S(1)} %bitcast.9, f32[2]{0:T(128)S(1)} %copy-done.4), custom_call_target="tpu_custom_call" | custom-call | tf_op jit(solution)/shard_map/pallas_call | solution.py:307
  60.8 0.7 %copy.7 = f32[6,4]{0,1:T(4,128)} copy(f32[6,4]{1,0:T(8,128)S(1)} %get-tuple-element.7) | data formatting | bytes 192
  61.5 0.7 %copy.9 = bf16[512,128]{1,0:T(8,128)(2,1)} copy(bf16[512,128]{1,0:T(8,128)(2,1)S(1)} %bitcast.8) | data formatting | bytes 262144
Async XLA Ops:
  0.6 1.4 %copy-start = (bf16[1,4,2,6,128,128]{5,4,3,2,1,0:T(8,128)(2,1)S(1)}, bf16[1,4,2,6,128,128]{5,4,3,2,1,0:T(8,128)(2,1)}, u32[]{:S(2)}) copy-start(bf16[1,4,2,6,128,128]{5,4,3,2,1,0:T(8,128)(2,1)} %param.7) | copy-start | bytes 4718596
  2.0 0.9 %copy-start.1 = (bf16[1,4,2,128,128]{4,3,2,1,0:T(8,128)(2,1)S(1)}, bf16[1,4,2,128,128]{4,3,2,1,0:T(8,128)(2,1)}, u32[]{:S(2)}) copy-start(bf16[1,4,2,128,128]{4,3,2,1,0:T(8,128)(2,1)} %param.6) | copy-start | bytes 786436
  3.0 0.9 %copy-start.2 = (bf16[512,128]{1,0:T(8,128)(2,1)S(1)}, bf16[512,128]{1,0:T(8,128)(2,1)}, u32[]{:S(2)}) copy-start(bf16[512,128]{1,0:T(8,128)(2,1)} %probes_ref.1) | copy-start | bytes 393220
  3.9 0.7 %copy-start.3 = (s32[1,4,2]{1,2,0:T(2,128)S(1)}, s32[1,4,2]{1,2,0:T(2,128)}, u32[]{:S(2)}) copy-start(s32[1,4,2]{1,2,0:T(2,128)} %param.8) | copy-start | bytes 100
  4.6 0.7 %copy-start.4 = (f32[2]{0:T(128)S(1)}, f32[2]{0:T(128)}, u32[]{:S(2)}) copy-start(f32[2]{0:T(128)} %coeffs_ref.1) | copy-start | bytes 28

commit v3 on v2

--- a/solution.py
+++ b/solution.py
@@ -14,7 +14,7 @@
     n_row,
     probes_ref, ham_ref, strain_ref, cols_ref, coeffs_ref,
     out_ref, stress_ref,
-    hbuf, pbuf, xbuf, cbuf, csm, coeffs, sbuf, strain_buf, x0t, x1t, x2t, dsend, dmine,
+    hbuf, mbuf, pbuf, xbuf, cbuf, csm, coeffs, sbuf, strain_buf, x0t, x1t, x2t, dsend, dmine,
     hs, hr, ps, pr, xs, xr, cs, cr, das, dar, dbs, dbr, ss, sr, loc,
 ):
     n_col = 4
@@ -35,14 +35,14 @@
     def dev(row, col):
         return (grp, row, col)
 
-    def others():
-        for d in range(1, nb):
-            k = (me + d) % nb
-            yield d, k
-
     barrier = pltpu.get_barrier_semaphore()
-    for _, k in others():
+
+    def greet(d, carry):
+        k = (me + d) % nb
         pl.semaphore_signal(barrier, inc=1, device_id=dev(k // n_col, k % n_col), device_id_type=MESH)
+        return carry
+
+    lax.fori_loop(1, nb, greet, 0)
     own = pl.ds(pl.multiple_of(me * sub, sub), sub)
     local_copies = [
         pltpu.make_async_copy(src, dst, loc.at[n])
@@ -77,13 +77,33 @@
                 copy.start()
         waits.append((copy, pred))
 
-    def small(src_of, dst, send, recv, place=lambda k: (k // n_col, k % n_col)):
-        for d, k in others():
-            launch(remote(src_of(k), dst, send.at[d], recv.at[me], dev(*place(k))))
+    sent_small = []
+
+    def small(src_of, dst, send, recv):
+        def copy_to(d):
+            k = (me + d) % nb
+            return remote(src_of(k), dst, send.at[d], recv.at[me], dev(k // n_col, k % n_col))
+
+        def go(t, carry):
+            copy_to((t + nb // 2) % nb).start()
+            return carry
+
+        lax.fori_loop(0, nb // 2, go, 0)
+
+        def rest(t, carry):
+            copy_to(t).start()
+            return carry
+
+        lax.fori_loop(1, nb // 2, rest, 0)
+        sent_small.append(copy_to)
 
     def small_wait(dst, send, recv):
-        for d, k in others():
+        def arrived(d, carry):
+            k = (me + d) % nb
             remote(dst.at[k], dst.at[k], send.at[d], recv.at[k], dev(z, sib)).wait_recv()
+            return carry
+
+        lax.fori_loop(1, nb, arrived, 0)
 
     small(lambda k: cols_ref, cbuf.at[me], cs, cr)
     small(lambda k: probes_ref.at[pl.ds(pl.multiple_of(k * sub, sub), sub)], xbuf.at[me], xs, xr)
@@ -176,8 +196,12 @@
     cols_copy.start()
     small_wait(xbuf, xs, xr)
     local_copies[1].wait()
-    for j in range(nb):
+
+    def turn(j, carry):
         x0t[j] = xbuf[j].astype(jnp.float32).T.astype(jnp.bfloat16)
+        return carry
+
+    lax.fori_loop(0, nb, turn, 0, unroll=4)
     cols_copy.wait()
     local_copies[2].wait()
 
@@ -185,11 +209,14 @@
         wave(d, ham_send, ham_recv, chunks)
     local_copies[3].wait()
     last(ham_recv, chunks)
-
     wave(1, probe_send, probe_recv, 1)
 
     def col_of(i, s):
         return jnp.clip(csm[i, s % cap, s // cap], 0, nb - 1)
+
+    def mirrored(a, g):
+        way = (a - g) % n_row
+        return way == 1 or (way == 2 and g in (0, n_row - 1))
 
     def mirror(a, g):
         def one_row(w, carry):
@@ -201,52 +228,75 @@
                 for t in range(1, cap):
                     place = jnp.where(csm[j, t, a] == i, t, place)
                 block = hbuf[j, a, place].T
-                hbuf[i, g, s] = jnp.where(raw >= 0, block, jnp.zeros_like(block))
+                mbuf[i, g, s] = jnp.where(raw >= 0, block, jnp.zeros_like(block))
             return carry
 
         lax.fori_loop(0, n_col, one_row, 0, unroll=True)
 
-    for g in range(groups):
-        mirror((g + 1) % groups, g)
-        if g in (0, n_row - 1):
-            mirror((g + 2) % groups, g)
+        def put_back(w, carry):
+            hbuf[a * n_col + w, g] = mbuf[a * n_col + w, g]
+            return carry
+
+        return lambda: lax.fori_loop(0, n_col, put_back, 0)
 
     def product(x_ref, i):
         weights = jnp.concatenate([x_ref[col_of(i, s)] for s in range(slots)], axis=0)
         rows = jnp.concatenate([hbuf[i, s // cap, s % cap] for s in range(slots)], axis=1)
         return jnp.dot(rows, weights, preferred_element_type=jnp.float32)
 
-    def one(i, carry):
+    def each_row(body):
+        def step(i, carry):
+            body(i)
+            return carry
+
+        lax.fori_loop(0, nb, step, 0, unroll=4)
+
+    def one(i):
         x1t[i] = product(x0t, i).astype(jnp.bfloat16)
-        return carry
-
-    def two(i, carry):
+
+    def two(i):
         x2t[i] = (2.0 * product(x1t, i) - x0t[i].astype(jnp.float32)).astype(jnp.bfloat16)
-        return carry
 
     mine_out = c * n_row + z
 
-    def density_copies(k):
-        return (
-            (k != me, remote(dsend.at[k], dmine.at[me], das.at[k], dar.at[me], dev(k // n_col, k % n_col))),
-            (k != mine_out, remote(dsend.at[k], out_ref.at[me], dbs.at[k], dbr.at[me], dev(k % n_row, k // n_row))),
+    def to_pair(k):
+        return k != me, remote(
+            dsend.at[k], dmine.at[me], das.at[k], dar.at[me], dev(k // n_col, k % n_col)
         )
 
-    def three(t, carry):
-        i = (me + 1 + t) % nb
+    def to_out(k):
+        return k != mine_out, remote(
+            dsend.at[k], out_ref.at[me], dbs.at[k], dbr.at[me], dev(k % n_row, k // n_row)
+        )
+
+    def three(i):
         prior = x1t[i].astype(jnp.float32)
         third = 2.0 * product(x2t, i) - prior
         dense = coeffs[0] * prior + coeffs[1] * third
         dsend[i] = dense.T.astype(jnp.bfloat16)
-        for pred, copy in density_copies(i):
-            pl.when(pred)(copy.start)
+
+    backs = [mirror(a, g) for a in range(n_row) for g in range(groups) if mirrored(a, g)]
+    for back in backs:
+        back()
+    each_row(one)
+    wave(2, probe_send, probe_recv, 1)
+    each_row(two)
+    wave(3, probe_send, probe_recv, 1)
+    each_row(three)
+
+    def start_pair(t, carry):
+        row = (z + 2 + t // n_col) % n_row
+        pred, copy = to_pair(row * n_col + (c + t) % n_col)
+        pl.when(pred)(copy.start)
         return carry
 
-    lax.fori_loop(0, nb, one, 0, unroll=2)
-    wave(2, probe_send, probe_recv, 1)
-    lax.fori_loop(0, nb, two, 0, unroll=2)
-    wave(3, probe_send, probe_recv, 1)
-    lax.fori_loop(0, nb, three, 0)
+    def start_out(k, carry):
+        pred, copy = to_out(k)
+        pl.when(pred)(copy.start)
+        return carry
+
+    lax.fori_loop(0, nb, start_pair, 0)
+    lax.fori_loop(0, nb, start_out, 0)
     dmine[me] = dsend[me]
     out_ref[me] = dsend[mine_out]
     for d in range(4, n_row + 1):
@@ -259,8 +309,8 @@
     dens = dmine[...].reshape(nb * sub, dmine.shape[2])
     dens_t = dens.astype(jnp.float32).T.astype(jnp.bfloat16)
     lane = lax.broadcasted_iota(jnp.int32, (comps, 128), 1)
-    part = jnp.zeros((comps, 128), jnp.float32)
-    for s in range(slots):
+
+    def pair(s, part):
         col = col_of(me, s)
         tile = jnp.dot(dens_t, pbuf[col], preferred_element_type=jnp.float32)
         sums = jnp.concatenate(
@@ -270,12 +320,24 @@
             ],
             axis=0,
         )
-        part = part + jnp.where(lane == col, jnp.sum(sums, axis=1, keepdims=True), 0.0)
+        return part + jnp.where(lane == col, jnp.sum(sums, axis=1, keepdims=True), 0.0)
+
+    part = lax.fori_loop(0, slots, pair, jnp.zeros((comps, 128), jnp.float32), unroll=2)
     sbuf[me] = jnp.concatenate([part, jnp.zeros((sbuf.shape[1] - comps, 128), jnp.float32)], axis=0)
     small(lambda k: sbuf.at[me], sbuf.at[me], ss, sr)
-    for k in range(nb):
-        for pred, copy in density_copies(k):
+    def sent(k, carry):
+        for pred, copy in (to_pair(k), to_out(k)):
             pl.when(pred)(copy.wait_send)
+        return carry
+
+    lax.fori_loop(0, nb, sent, 0)
+
+    def sent_others(d, carry):
+        for copy_to in sent_small:
+            copy_to(d).wait_send()
+        return carry
+
+    lax.fori_loop(1, nb, sent_others, 0)
     for copy, pred in waits:
         if pred is None:
             copy.wait_send()
@@ -313,6 +375,7 @@
         in_specs=[hbm] * 5,
         out_specs=(vmem, vmem),
         scratch_shapes=[
+            pltpu.VMEM((nb, groups, cap, block, block), bf16),
             pltpu.VMEM((nb, groups, cap, block, block), bf16),
             pltpu.VMEM((nb, probe_count, block), bf16),
             pltpu.VMEM((nb, sub, block), bf16),
@@ -336,7 +399,7 @@
             dma((7,)),
         ],
         compiler_params=pltpu.CompilerParams(
-            collective_id=0, has_side_effects=True, vmem_limit_bytes=40 * 1024 * 1024
+            collective_id=0, has_side_effects=True, vmem_limit_bytes=64 * 1024 * 1024 - 65536
         ),
     )(
         probes,

time: 62.3 us -> 60.3 us (0.968)
  local copies, waits for them, and re-layouts: 5.91 us -> 2.91 us
  Pallas kernels: 55.6 us -> 56.5 us
    unnamed x12 -> x2, local copies, waits for them, and re-layouts: 5.91 us -> 2.91 us
    pallas_call x1, Pallas kernels: 55.6 us -> 56.5 us  [fused_local(): pl.pallas_call(functools.partial(fused_kernel, n_row), out_shape=(jax.Sha...]
where the time goes in v3:
time: 60.3 us; the launch traced here: 60.1 us
  Pallas kernels  56.5 us (94%)
  local copies, waits for them, and re-layouts  2.91 us (5%)
  between operations  0.64 us (1%)
    pallas_call x1, Pallas kernels, fused_local(): pl.pallas_call(functools.partial(fused_kernel, n_row), out_shape=(jax.Sha...  56.5 us
    unnamed x2, local copies, waits for them, and re-layouts  2.91 us

profile of v3, /device:TPU:0, one launch (start us, length us, event | category | flops | bytes accessed | tf_op | source)
XLA Modules:
  0.0 60.1 jit_solution(7723652646526836564)
XLA Ops:
  0.6 56.5 %shard_map.68 = (bf16[16,32,128]{2,1,0:T(8,128)(2,1)}, f32[6,4]{1,0:T(8,128)}) custom-call(bf16[512,128]{1,0:T(8,128)(2,1)} %probes_ref.1, bf16[4,2,128,128]{3,2,1,0:T(8,128)(2,1)} %bitcast.7, bf16[8,6,128,128]{3,2,1,0:T(8,128)(2,1)} %bitcast.6, s32[2,4]{1,0:T(2,128)} %bitcast.9, f32[2]{0:T(128)} %coeffs_ref.1), custom_call_target="tpu_custom_call" | custom-call | tf_op jit(solution)/shard_map/pallas_call | solution.py:369
  57.1 1.3 %copy.7 = f32[6,4]{0,1:T(4,128)} copy(f32[6,4]{1,0:T(8,128)} %get-tuple-element.7) | data formatting | bytes 192
  58.5 1.6 %copy.9 = bf16[512,128]{1,0:T(8,128)(2,1)} copy(bf16[512,128]{1,0:T(8,128)(2,1)} %bitcast.8) | data formatting | bytes 262144

commit v4 on v3

--- a/solution.py
+++ b/solution.py
@@ -136,12 +136,18 @@
             def _():
                 copy.wait_recv()
 
+    half = probes_ref.shape[0] // 2
+
+    def probe_part(ref, m):
+        return ref.at[pl.ds(m * half, half)]
+
     def probe_send(org, m, way, target, pred=None):
-        src = probes_ref if org is me else pbuf.at[org]
-        launch(remote(src, pbuf.at[org], ps.at[org, way], pr.at[org], target), pred)
+        src = probe_part(probes_ref if org is me else pbuf.at[org], m)
+        launch(remote(src, probe_part(pbuf.at[org], m), ps.at[org, m, way], pr.at[org, m], target), pred)
 
     def probe_recv(org, m):
-        remote(pbuf.at[org], pbuf.at[org], ps.at[org, 0], pr.at[org], dev(z, sib)).wait_recv()
+        part = probe_part(pbuf.at[org], m)
+        remote(part, part, ps.at[org, m, 0], pr.at[org, m], dev(z, sib)).wait_recv()
 
     up, down = z + 1, z - 1
     has_up, has_down = z < n_row - 1, z > 0
@@ -187,8 +193,27 @@
                 recv(row * n_col + sib, m)
                 recv(row * n_col + ysib, m)
 
+    def chain(d):
+        for col in (c, yc):
+            for sgn in (-1, 1) if (d - (col is yc)) > 0 else (1,):
+                step = d - 1 if col is yc else d
+                if step > n_row - 1:
+                    continue
+                zo = z + sgn * step
+                ok = zo >= 0 if sgn < 0 else zo <= n_row - 1
+                org = jnp.clip(zo, 0, n_row - 1) * n_col + col
+
+                @pl.when(ok)
+                def _():
+                    probe_recv(org, 1)
+                if step < n_row - 1 and (sgn < 0 or step == 0):
+                    probe_send(org, 1, 0, dev(jnp.minimum(up, n_row - 1), c), jnp.logical_and(ok, has_up))
+                if step < n_row - 1 and (sgn > 0 or step == 0):
+                    probe_send(org, 1, 1, dev(jnp.maximum(down, 0), c), jnp.logical_and(ok, has_down))
+                probe_send(org, 1, 3, dev(z, sib), ok)
+
     first(ham_send, chunks)
-    first(probe_send, 1)
+    first(probe_send, 2)
 
     small_wait(cbuf, cs, cr)
     local_copies[0].wait()
@@ -210,6 +235,7 @@
     local_copies[3].wait()
     last(ham_recv, chunks)
     wave(1, probe_send, probe_recv, 1)
+    chain(1)
 
     def col_of(i, s):
         return jnp.clip(csm[i, s % cap, s // cap], 0, nb - 1)
@@ -280,8 +306,10 @@
         back()
     each_row(one)
     wave(2, probe_send, probe_recv, 1)
+    chain(2)
     each_row(two)
     wave(3, probe_send, probe_recv, 1)
+    chain(3)
     each_row(three)
 
     def start_pair(t, carry):
@@ -301,7 +329,8 @@
     out_ref[me] = dsend[mine_out]
     for d in range(4, n_row + 1):
         wave(d, probe_send, probe_recv, 1)
-    last(probe_recv, 1)
+        chain(d)
+    last(probe_recv, 2)
 
     small_wait(dmine, das, dar)
     local_copies[4].wait()
@@ -390,7 +419,7 @@
             pltpu.VMEM((nb, sub, block), bf16),
             pltpu.VMEM((nb, sub, block), bf16),
             dma((nb, chunks, 4)), dma((nb, chunks)),
-            dma((nb, 4)), dma((nb,)),
+            dma((nb, 2, 4)), dma((nb, 2)),
             dma((nb,)), dma((nb,)),
             dma((nb,)), dma((nb,)),
             dma((nb,)), dma((nb,)),

time: 60.3 us -> 59.9 us (level)
  no operation moved by 1% of the time
where the time goes in v4:
time: 59.9 us; the launch traced here: 59.7 us
  Pallas kernels  56.2 us (94%)
  local copies, waits for them, and re-layouts  2.91 us (5%)
  between operations  0.64 us (1%)
    pallas_call x1, Pallas kernels, fused_local(): pl.pallas_call(functools.partial(fused_kernel, n_row), out_shape=(jax.Sha...  56.2 us
    unnamed x2, local copies, waits for them, and re-layouts  2.91 us

profile of v4, /device:TPU:0, one launch (start us, length us, event | category | flops | bytes accessed | tf_op | source)
XLA Modules:
  0.0 59.7 jit_solution(6033598022963856508)
XLA Ops:
  0.6 56.2 %shard_map.68 = (bf16[16,32,128]{2,1,0:T(8,128)(2,1)}, f32[6,4]{1,0:T(8,128)}) custom-call(bf16[512,128]{1,0:T(8,128)(2,1)} %probes_ref.1, bf16[4,2,128,128]{3,2,1,0:T(8,128)(2,1)} %bitcast.7, bf16[8,6,128,128]{3,2,1,0:T(8,128)(2,1)} %bitcast.6, s32[2,4]{1,0:T(2,128)} %bitcast.9, f32[2]{0:T(128)} %coeffs_ref.1), custom_call_target="tpu_custom_call" | custom-call | tf_op jit(solution)/shard_map/pallas_call | solution.py:398
  56.8 1.3 %copy.7 = f32[6,4]{0,1:T(4,128)} copy(f32[6,4]{1,0:T(8,128)} %get-tuple-element.7) | data formatting | bytes 192
  58.2 1.6 %copy.9 = bf16[512,128]{1,0:T(8,128)(2,1)} copy(bf16[512,128]{1,0:T(8,128)(2,1)} %bitcast.8) | data formatting | bytes 262144
